TPU v7x, 256 devices: a whole 4x4x8 slice. The times are simulated.
256 devices in a mesh: blk: 16 (over y_hi, z), frames: 16 (over x, y_lo, core).
Axes of the slice: x: 4, y: 4 (y_hi: 2, y_lo: 2; y = y_hi * 2 + y_lo), z: 8, core: 2. Of those that a mesh axis runs over, the one named last changes fastest.
Arguments:
- coarse_query: bfloat16 [512, 16, 256], P('blk'), may hold values from -125 to 125
- coarse_feat: bfloat16 [64, 8160, 256], P('frames', 'blk'), may hold values from -61 to 61
- fine_query: bfloat16 [512, 128], P(('blk', 'frames')), may hold values from -175 to 175
- fine_tiles: bfloat16 [64, 1024, 64, 128], P('frames', 'blk'), may hold values from -61 to 61
- track_pos: int32 [2, 64, 512], P(None, None, ('blk', 'frames')), may hold values from 0 to 959, as said below
- tile_list: int32 [64, 16, 16, 8], P('frames', 'blk'), may hold values from 0 to 63, as said below
- tile_valid: int32 [64, 16, 16, 8], P('frames', 'blk'), may hold values from 0 to 1, as said below
Outputs:
- coarse_pos: float32 [2, 64, 512], P(None, 'frames', 'blk')
- fine_offset: float32 [2, 64, 512], P(None, None, ('blk', 'frames'))
Inputs may be any that keep to these rules, and one draw needn't show every extreme that they name: `tile_list`: in each list the valid slots come first and name distinct tiles of the group's window; padded slots hold 63; in every frame and group some owner's list is full. `tile_valid`: each list has at least 4 valid slots. `track_pos`: rows lie below 544 and columns below 960.
All inputs are finite; a program needn't handle non-finite values.
Results may differ from a plain program's by a relative error of at most 0.0003.
Values may be sent and summed in bfloat16 or wider, within the bound.
A program may use at most 192 MiB of HBM per device.

v0:
```python
import math
import jax
import jax.numpy as jnp
from jax import lax
from jax.sharding import PartitionSpec as P

GH = 68
GW = 120
TILE = 8
SPREAD = 32.0


def coarse(coarse_query, coarse_feat):
    track_group, heads, channels = coarse_query.shape
    frames_here, region, _ = coarse_feat.shape
    blocks = lax.axis_size("blk")
    scale = 1.0 / math.sqrt(channels)
    start = lax.axis_index("blk") * region
    queries = lax.all_gather(coarse_query.reshape(track_group * heads, channels), "blk", axis=0)
    positions = start + jnp.arange(region, dtype=jnp.int32)
    pos_row = (positions // GW).astype(jnp.float32)
    pos_col = (positions % GW).astype(jnp.float32)
    scores = (
        jnp.einsum("brc,fpc->bfpr", queries, coarse_feat, preferred_element_type=jnp.float32)
        * scale
    )
    top = jnp.max(scores, axis=2)
    weights = jnp.exp(scores - top[:, :, None])
    stats = jnp.stack(
        [
            top,
            jnp.sum(weights, axis=2),
            jnp.sum(weights * pos_row[None, None, :, None], axis=2),
            jnp.sum(weights * pos_col[None, None, :, None], axis=2),
        ],
        axis=1,
    )
    stats = lax.all_to_all(stats, "blk", split_axis=0, concat_axis=0, tiled=True)
    top = jnp.max(stats[:, 0], axis=0, keepdims=True)
    factor = jnp.exp(stats[:, 0] - top)
    total = jnp.sum(stats[:, 1] * factor, axis=0)
    rows = jnp.sum(stats[:, 2] * factor, axis=0) / total
    cols = jnp.sum(stats[:, 3] * factor, axis=0) / total
    rows = jnp.mean(rows.reshape(frames_here, track_group, heads), axis=2)
    cols = jnp.mean(cols.reshape(frames_here, track_group, heads), axis=2)
    return jnp.stack([(rows - (GH - 1) / 2.0) / (GH / 4.0), (cols - (GW - 1) / 2.0) / (GW / 4.0)])


def fine(fine_query, fine_tiles, track_pos, tile_list, tile_valid, region):
    frames_here, tiles, cells, channels = fine_tiles.shape
    owners = tile_list.shape[2]
    owned = fine_query.shape[0]
    start = lax.axis_index("blk") * region
    descs = lax.all_gather(fine_query, "frames", axis=0, tiled=True)
    places = lax.all_to_all(track_pos, "frames", split_axis=1, concat_axis=2, tiled=True).astype(
        jnp.float32
    )
    scores = jnp.einsum(
        "nc,fkc->fnk",
        descs,
        fine_tiles.reshape(frames_here, tiles * cells, channels),
        preferred_element_type=jnp.float32,
    ) * (1.0 / math.sqrt(channels))
    ids = tile_list[:, 0]
    live = tile_valid[:, 0]
    listed = jnp.any((ids[:, :, :, None] == jnp.arange(tiles)) & (live[:, :, :, None] > 0), axis=2)
    listed = jnp.repeat(jnp.repeat(listed, owned, axis=1), cells, axis=2)
    index = jnp.arange(tiles * cells, dtype=jnp.int32)
    cell = start + index // cells
    inner = index % cells
    row = (cell // GW * TILE + inner // TILE).astype(jnp.float32)
    col = (cell % GW * TILE + inner % TILE).astype(jnp.float32)
    away_row = row - places[0][:, :, None]
    away_col = col - places[1][:, :, None]
    scores = scores - (away_row**2 + away_col**2) * (0.5 / (SPREAD * SPREAD))
    scores = jnp.where(listed, scores, -1e30)
    weights = jnp.exp(scores - jnp.max(scores, axis=2, keepdims=True))
    total = jnp.sum(weights, axis=2)
    out = jnp.stack(
        [
            jnp.sum(weights * away_row, axis=2) / total / SPREAD,
            jnp.sum(weights * away_col, axis=2) / total / SPREAD,
        ]
    )
    return lax.all_to_all(out, "frames", split_axis=2, concat_axis=1, tiled=True)


def body(coarse_query, coarse_feat, fine_query, fine_tiles, track_pos, tile_list, tile_valid):
    offset = fine(fine_query, fine_tiles, track_pos, tile_list, tile_valid, coarse_feat.shape[1])
    return (coarse(coarse_query, coarse_feat), offset)


def solution(mesh):
    return jax.shard_map(
        body,
        mesh=mesh,
        in_specs=(
            P("blk", None, None),
            P("frames", "blk", None),
            P(("blk", "frames"), None),
            P("frames", "blk", None, None),
            P(None, None, ("blk", "frames")),
            P("frames", "blk", None, None),
            P("frames", "blk", None, None),
        ),
        out_specs=(P(None, "frames", "blk"), P(None, None, ("blk", "frames"))),
        check_vma=False,
    )
```

profile of v0, /device:TPU:2, one launch (start us, length us, event | category | flops | bytes accessed | tf_op | source)
XLA Modules:
  0.0 203.0 jit_solution(1856049340781756826)
XLA Ops:
  7.2 0.0 all-gather.3.cloned.1.call-start
  7.2 0.7 all-gather.3.cloned.1.call-update
  7.9 1.4 copy.87
  9.3 5.9 %all-to-all-start.1 = ((s32[2,64,2]{2,0,1:T(2,128)}), s32[2,64,2]{2,0,1:T(2,128)S(1)}, u32[]{:S(2)}, u32[]{:S(2)}) async-start(s32[2,64,2]{2,0,1:T(2,128)} %copy.87), calls=%async_computation.1 | async-start | bytes 131072 | tf_op jit(solution)/shard_map/all_to_all | solution.py:55
  15.2 0.8 copy.83
  16.0 0.7 compare_bitcast_fusion
  16.7 0.1 copy.84
  16.8 0.2 fusion.16
  17.1 17.5 %all-gather = bf16[16,2,128]{2,1,0:T(2,128)(2,1)S(1)} all-gather(bf16[1,2,128]{2,1,0:T(2,128)(2,1)} %bitcast.111), channel_id=1, replica_groups=mesh['blk'=16,'frames'=16] {'frames'}, dimensions={0}, use_global_device_ids=true | all-gather | bytes 8704 | tf_op jit(solution)/shard_map/all_gather | solution.py:54
  34.6 1.4 broadcast_in_dim.9
  36.0 2.6 %reshape.202 = pred[4,32,4096]{2,1,0:T(32,128)(4,1)S(1)} reshape(pred[4,32,64,64]{3,2,1,0:T(32,128)(4,1)S(1)} %broadcast_in_dim.9) | data formatting | bytes 1048576 | tf_op jit(solution)/shard_map/reshape | solution.py:67
  38.6 0.0 all-to-all-done.1
  38.6 0.1 copy.88
  38.7 0.1 convert_element_type.42
  38.8 0.1 copy.90
  38.9 0.1 copy.92
  39.0 0.0 copy-start
  39.0 4.6 %fusion.12 = (f32[4,32]{1,0:T(4,128)S(1)}, f32[4,32]{1,0:T(4,128)S(1)}, f32[4,32]{1,0:T(4,128)S(1)}) fusion(f32[4,32]{1,0:T(4,128)S(1)} %copy.90, f32[4096]{0:T(1024)S(1)} %get-tuple-element.19, f32[4,32]{1,0:T(4,128)S(1)} %copy.92, f32[4096]{0:T(1024)S(1)} %get-tuple-element.20, pred[4,32,4096]{2,1,0:T(32,128)(4,1)S(1)} %reshape.202, ...), kind=kOutput, calls=%fused_computation.21 | convolution fusion | flops 143134464 | bytes 4762112 | tf_op jit(solution)/shard_map/sub | solution.py:77
  43.6 0.7 copy.93
  44.3 6.0 %all-to-all-start.2 = ((f32[2,4,32]{1,0,2:T(2,128)}), f32[2,4,32]{1,0,2:T(2,128)S(1)}, u32[]{:S(2)}, u32[]{:S(2)}) async-start(f32[2,4,32]{1,0,2:T(2,128)} %copy.93), calls=%async_computation.2 | async-start | bytes 65536 | tf_op jit(solution)/shard_map/all_to_all | solution.py:85
  50.3 63.3 %all-gather.3.cloned.1.call-done = bf16[16,512,256]{2,1,0:T(8,128)(2,1)} async-done(((bf16[1,512,256]{2,1,0:T(8,128)(2,1)}), bf16[16,512,256]{2,1,0:T(8,128)(2,1)}) %all-gather.3.cloned.1.call-update) | async-done | bytes 4194320 | tf_op jit(solution)/shard_map/all_gather | solution.py:19
  113.6 0.0 copy-done
  113.6 25.3 %bitcast_reduce_fusion = (f32[16,4,512]{2,0,1:T(8,128)S(1)}, f32[4,510,16,512]{3,1,2,0:T(8,128)}) fusion(bf16[16,512,256]{2,1,0:T(8,128)(2,1)} %all-gather.3.cloned.1.call-done, bf16[4,510,256,1]{2,0,1,3:T(4,128)(2,1)S(1)} %bitcast.99), kind=kOutput, calls=%fused_computation.2 | convolution fusion | flops 8589770752 | bytes 72216576 | tf_op jit(solution)/shard_map/brc,fpc->bfpr/dot_general | solution.py:24
  138.9 36.5 %fusion.2 = (f32[16,4,512]{2,0,1:T(8,128)S(1)}, f32[16,4,512]{2,0,1:T(8,128)S(1)}, f32[16,4,512]{2,0,1:T(8,128)S(1)}) fusion(f32[4,510,16,512]{3,1,2,0:T(8,128)} %get-tuple-element.18, f32[16,4,512]{2,0,1:T(8,128)S(1)} %get-tuple-element.17, f32[510]{0:T(512)S(1)} %get-tuple-element.22, f32[510]{0:T(512)S(1)} %get-tuple-element.21), kind=kLoop, calls=%fused_computation.6 | loop fusion | flops 116883456 | bytes 67375088 | tf_op jit(solution)/shard_map/reduce_sum | solution.py:32
  175.5 1.1 copy.79
  176.7 0.0 all-to-all-done.2
  176.7 4.2 %all-to-all-start = ((f32[16,4,4,512]{3,2,1,0:T(4,128)}), f32[16,4,4,512]{3,2,1,0:T(4,128)S(1)}, u32[]{:S(2)}, u32[]{:S(2)}) async-start(f32[16,4,4,512]{3,2,1,0:T(4,128)} %copy.79), calls=%async_computation | async-start | bytes 1048576 | tf_op jit(solution)/shard_map/all_to_all | solution.py:38
  180.9 0.7 all_to_all.28
  181.5 13.4 %all-to-all-done = f32[16,4,4,512]{3,2,1,0:T(4,128)S(1)} async-done(((f32[16,4,4,512]{3,2,1,0:T(4,128)}), f32[16,4,4,512]{3,2,1,0:T(4,128)S(1)}, u32[]{:S(2)}, u32[]{:S(2)}) %all-to-all-start) | async-done | bytes 524320 | tf_op jit(solution)/shard_map/all_to_all | solution.py:38
  195.0 0.1 fusion.22
  195.1 0.1 div.112
  195.2 0.1 reduce_sum.106
  195.3 0.1 div.106
  195.4 0.1 reduce_sum.104
  195.5 0.6 pad_maximum_fusion.1
  (18 shorter events, 0.2 us)
Async XLA Ops:
  7.2 106.4 %all-gather.3.cloned.1.call-start = ((), (), s32[]{:S(2)}) async-start(), calls=%async_computation.3 | async-start | bytes 4456448 | tf_op jit(solution)/shard_map/all_gather | solution.py:19
  9.3 29.3 %all-to-all-start.1 = ((s32[2,64,2]{2,0,1:T(2,128)}), s32[2,64,2]{2,0,1:T(2,128)S(1)}, u32[]{:S(2)}, u32[]{:S(2)}) async-start(s32[2,64,2]{2,0,1:T(2,128)} %copy.87), calls=%async_computation.1 | async-start | bytes 131072 | tf_op jit(solution)/shard_map/all_to_all | solution.py:55
  39.0 74.6 %copy-start = (bf16[4,510,256]{2,0,1:T(4,128)(2,1)S(1)}, bf16[4,510,256]{2,0,1:T(4,128)(2,1)}, u32[]{:S(2)}) copy-start(bf16[4,510,256]{2,0,1:T(4,128)(2,1)} %param.8) | copy-start | bytes 3133444
  44.3 132.3 %all-to-all-start.2 = ((f32[2,4,32]{1,0,2:T(2,128)}), f32[2,4,32]{1,0,2:T(2,128)S(1)}, u32[]{:S(2)}, u32[]{:S(2)}) async-start(f32[2,4,32]{1,0,2:T(2,128)} %copy.93), calls=%async_computation.2 | async-start | bytes 65536 | tf_op jit(solution)/shard_map/all_to_all | solution.py:85
  176.7 18.3 %all-to-all-start = ((f32[16,4,4,512]{3,2,1,0:T(4,128)}), f32[16,4,4,512]{3,2,1,0:T(4,128)S(1)}, u32[]{:S(2)}, u32[]{:S(2)}) async-start(f32[16,4,4,512]{3,2,1,0:T(4,128)} %copy.79), calls=%async_computation | async-start | bytes 1048576 | tf_op jit(solution)/shard_map/all_to_all | solution.py:38
Sparse Core Ops, SparseCore 0:
  10.6 102.9 all-gather.2
where the time goes:
time: 203 us
  waiting for transfers between devices  77.4 us (38%)
  other arithmetic  38.6 us (19%)
  matrix products  29.9 us (15%)
  blocking collectives  17.5 us (9%)
  starting transfers between devices  16.1 us (8%)
  between operations  14.2 us (7%)
  local copies, waits for them, and re-layouts  9.39 us (5%)
    all_gather x1, waiting for transfers between devices, coarse(): lax.all_gather(coarse_query.reshape(track_group * heads, channels), 'blk'...  63.3 us
    reduce_sum x1, other arithmetic, coarse(): jnp.sum(weights, axis=2)  36.5 us
    dot_general x1, matrix products, coarse(): jnp.einsum('brc,fpc->bfpr', queries, coarse_feat, preferred_element_type=...  25.3 us
    all_gather x1, blocking collectives, fine(): descs = lax.all_gather(fine_query, 'frames', axis=0, tiled=True)  17.5 us
    all_to_all x1, waiting for transfers between devices, coarse(): lax.all_to_all(stats, 'blk', split_axis=0, concat_axis=0, tiled=True)  13.4 us
    all_to_all x1, starting transfers between devices, fine(): lax.all_to_all(out, 'frames', split_axis=2, concat_axis=1, tiled=True)  5.99 us
    all_to_all x1, starting transfers between devices, fine(): lax.all_to_all(track_pos, 'frames', split_axis=1, concat_axis=2, tiled=True)  5.86 us
    sub x1, matrix products, fine(): weights = jnp.exp(scores - jnp.max(scores, axis=2, keepdims=True))  4.61 us
  transfers between devices with their start and end apart: 4, of which 2 were waited for; matrix products, arithmetic and copies ran while one was open for 37% of the time, Pallas kernels for 0%

commit v1 on v0

--- a/solution.py
+++ b/solution.py
@@ -8,6 +8,18 @@
 GW = 120
 TILE = 8
 SPREAD = 32.0
+
+
+def tables_check(slab_in, axis_name="frames"):
+    return jnp.concatenate(
+        lax.all_to_all(
+            jnp.stack(jnp.split(slab_in, lax.axis_size(axis_name), axis=2)),
+            concat_axis=0,
+            axis_name=axis_name,
+            split_axis=0,
+        ),
+        1,
+    )
 
 
 def coarse(coarse_query, coarse_feat):
@@ -82,7 +94,7 @@
             jnp.sum(weights * away_col, axis=2) / total / SPREAD,
         ]
     )
-    return lax.all_to_all(out, "frames", split_axis=2, concat_axis=1, tiled=True)
+    return tables_check(out)
 
 
 def body(coarse_query, coarse_feat, fine_query, fine_tiles, track_pos, tile_list, tile_valid):

time: 203 us -> 204 us (level)
  local copies, waits for them, and re-layouts: 9.39 us -> 19.6 us
  waiting for transfers between devices: 77.4 us -> 67.8 us
    all_gather x1, waiting for transfers between devices: 63.3 us -> 53.2 us  [coarse(): lax.all_gather(coarse_query.reshape(track_group * heads, channels), 'blk'...]
    unnamed x3 -> x18, local copies, waits for them, and re-layouts: 1.41 us -> 10.2 us
  transfers between devices with their start and end apart: 4 -> 4, of which waited for: 2 -> 2; matrix products, arithmetic and copies ran while one was open for 37% -> 43% of each run, Pallas kernels for 0% -> 0%
where the time goes in v1:
time: 204 us
  waiting for transfers between devices  67.8 us (33%)
  other arithmetic  38.6 us (19%)
  matrix products  30 us (15%)
  local copies, waits for them, and re-layouts  19.6 us (10%)
  blocking collectives  17.5 us (9%)
  starting transfers between devices  16.1 us (8%)
  between operations  14.2 us (7%)
    all_gather x1, waiting for transfers between devices, coarse(): lax.all_gather(coarse_query.reshape(track_group * heads, channels), 'blk'...  53.2 us
    reduce_sum x1, other arithmetic, coarse(): jnp.sum(weights, axis=2)  36.4 us
    dot_general x1, matrix products, coarse(): jnp.einsum('brc,fpc->bfpr', queries, coarse_feat, preferred_element_type=...  25.3 us
    all_gather x1, blocking collectives, fine(): descs = lax.all_gather(fine_query, 'frames', axis=0, tiled=True)  17.5 us
    all_to_all x1, waiting for transfers between devices, coarse(): lax.all_to_all(stats, 'blk', split_axis=0, concat_axis=0, tiled=True)  13.9 us
    unnamed x18, local copies, waits for them, and re-layouts  10.2 us
    all_to_all x1, starting transfers between devices, tables_check(): lax.all_to_all(jnp.stack(jnp.split(slab_in, lax.axis_size(axis_name), axi...  5.99 us
    all_to_all x1, starting transfers between devices, fine(): lax.all_to_all(track_pos, 'frames', split_axis=1, concat_axis=2, tiled=True)  5.86 us
  transfers between devices with their start and end apart: 4, of which 2 were waited for; matrix products, arithmetic and copies ran while one was open for 43% of the time, Pallas kernels for 0%

profile of v1, /device:TPU:2, one launch (start us, length us, event | category | flops | bytes accessed | tf_op | source)
XLA Modules:
  0.0 203.7 jit_solution(10711308256486588614)
XLA Ops:
  7.2 0.7 all-gather.3.cloned.1.call-update
  7.9 1.4 copy.192
  9.3 5.9 %all-to-all-start.1 = ((s32[2,64,2]{2,0,1:T(2,128)}), s32[2,64,2]{2,0,1:T(2,128)S(1)}, u32[]{:S(2)}, u32[]{:S(2)}) async-start(s32[2,64,2]{2,0,1:T(2,128)} %copy.192), calls=%async_computation.1 | async-start | bytes 131072 | tf_op jit(solution)/shard_map/all_to_all | solution.py:67
  15.2 0.8 copy.188
  16.0 0.7 compare_bitcast_fusion
  16.8 0.2 fusion.16
  17.1 17.5 %all-gather = bf16[16,2,128]{2,1,0:T(2,128)(2,1)S(1)} all-gather(bf16[1,2,128]{2,1,0:T(2,128)(2,1)} %bitcast.141), channel_id=1, replica_groups=mesh['blk'=16,'frames'=16] {'frames'}, dimensions={0}, use_global_device_ids=true | all-gather | bytes 8704 | tf_op jit(solution)/shard_map/all_gather | solution.py:66
  34.6 1.4 broadcast_in_dim.9
  36.0 2.7 %reshape.208 = pred[4,32,4096]{2,1,0:T(32,128)(4,1)S(1)} reshape(pred[4,32,64,64]{3,2,1,0:T(32,128)(4,1)S(1)} %broadcast_in_dim.9) | data formatting | bytes 1048576 | tf_op jit(solution)/shard_map/reshape | solution.py:79
  39.0 4.6 %fusion.13 = (f32[4,32]{1,0:T(4,128)S(1)}, f32[4,32]{1,0:T(4,128)S(1)}, f32[4,32]{1,0:T(4,128)S(1)}) fusion(f32[4,32]{1,0:T(4,128)S(1)} %copy.197, f32[4096]{0:T(1024)S(1)} %get-tuple-element.36, f32[4,32]{1,0:T(4,128)S(1)} %copy.195, f32[4096]{0:T(1024)S(1)} %get-tuple-element.35, pred[4,32,4096]{2,1,0:T(32,128)(4,1)S(1)} %reshape.208, ...), kind=kOutput, calls=%fused_computation.22 | convolution fusion | flops 143134464 | bytes 4762112 | tf_op jit(solution)/shard_map/sub | solution.py:89
  43.8 0.1 copy.198
  43.9 0.1 copy.199
  44.0 0.1 copy.200
  44.1 0.1 copy.201
  44.2 0.1 copy.202
  44.3 0.1 copy.203
  44.6 0.1 copy.206
  44.7 0.1 copy.207
  44.8 0.1 copy.208
  44.9 0.1 copy.209
  45.0 0.1 copy.210
  45.1 0.1 copy.211
  45.4 0.6 constant_dynamic-update-slice_fusion.15
  46.0 0.6 constant_dynamic-update-slice_fusion.14
  46.6 0.6 constant_dynamic-update-slice_fusion.13
  47.2 0.6 constant_dynamic-update-slice_fusion.12
  47.8 0.6 constant_dynamic-update-slice_fusion.11
  48.4 0.6 constant_dynamic-update-slice_fusion.10
  49.0 0.6 constant_dynamic-update-slice_fusion.9
  49.5 0.6 constant_dynamic-update-slice_fusion.8
  50.1 0.6 constant_dynamic-update-slice_fusion.7
  50.7 0.6 constant_dynamic-update-slice_fusion.6
  51.3 0.6 constant_dynamic-update-slice_fusion.5
  51.8 0.6 constant_dynamic-update-slice_fusion.4
  52.4 0.6 constant_dynamic-update-slice_fusion.3
  53.0 0.6 constant_dynamic-update-slice_fusion.2
  53.6 0.6 constant_dynamic-update-slice_fusion.1
  54.2 0.6 constant_dynamic-update-slice_fusion
  54.8 6.0 %all-to-all-start.2 = ((f32[16,2,4,2]{2,3,1,0:T(2,128)}), f32[16,2,4,2]{2,3,1,0:T(2,128)S(1)}, u32[]{:S(2)}, u32[]{:S(2)}) async-start(f32[16,2,4,2]{2,3,1,0:T(2,128)} %constant_dynamic-update-slice_fusion), calls=%async_computation.2 | async-start | bytes 65536 | tf_op jit(solution)/shard_map/all_to_all | solution.py:15
  60.8 53.2 %all-gather.3.cloned.1.call-done = bf16[16,512,256]{2,1,0:T(8,128)(2,1)} async-done(((bf16[1,512,256]{2,1,0:T(8,128)(2,1)}), bf16[16,512,256]{2,1,0:T(8,128)(2,1)}) %all-gather.3.cloned.1.call-update) | async-done | bytes 4194320 | tf_op jit(solution)/shard_map/all_gather | solution.py:31
  113.9 25.3 %bitcast_reduce_fusion = (f32[16,4,512]{2,0,1:T(8,128)S(1)}, f32[4,510,16,512]{3,1,2,0:T(8,128)}) fusion(bf16[16,512,256]{2,1,0:T(8,128)(2,1)} %all-gather.3.cloned.1.call-done, bf16[4,510,256,1]{2,0,1,3:T(4,128)(2,1)S(1)} %bitcast.129), kind=kOutput, calls=%fused_computation.2 | convolution fusion | flops 8589770752 | bytes 72216576 | tf_op jit(solution)/shard_map/brc,fpc->bfpr/dot_general | solution.py:36
  139.3 36.4 %fusion.2 = (f32[16,4,512]{2,0,1:T(8,128)S(1)}, f32[16,4,512]{2,0,1:T(8,128)S(1)}, f32[16,4,512]{2,0,1:T(8,128)S(1)}) fusion(f32[4,510,16,512]{3,1,2,0:T(8,128)} %get-tuple-element.34, f32[16,4,512]{2,0,1:T(8,128)S(1)} %get-tuple-element.33, f32[510]{0:T(512)S(1)} %get-tuple-element.38, f32[510]{0:T(512)S(1)} %get-tuple-element.37), kind=kLoop, calls=%fused_computation.6 | loop fusion | flops 116883456 | bytes 67375088 | tf_op jit(solution)/shard_map/reduce_sum | solution.py:44
  175.7 1.1 copy.184
  176.9 4.2 %all-to-all-start = ((f32[16,4,4,512]{3,2,1,0:T(4,128)}), f32[16,4,4,512]{3,2,1,0:T(4,128)S(1)}, u32[]{:S(2)}, u32[]{:S(2)}) async-start(f32[16,4,4,512]{3,2,1,0:T(4,128)} %copy.184), calls=%async_computation | async-start | bytes 1048576 | tf_op jit(solution)/shard_map/all_to_all | solution.py:50
  181.1 0.7 reshape.211
  181.8 13.9 %all-to-all-done = f32[16,4,4,512]{3,2,1,0:T(4,128)S(1)} async-done(((f32[16,4,4,512]{3,2,1,0:T(4,128)}), f32[16,4,4,512]{3,2,1,0:T(4,128)S(1)}, u32[]{:S(2)}, u32[]{:S(2)}) %all-to-all-start) | async-done | bytes 524320 | tf_op jit(solution)/shard_map/all_to_all | solution.py:50
  195.7 0.1 fusion.22
  196.3 0.6 pad_maximum_fusion.2
  (36 shorter events, 1.6 us)
Async XLA Ops:
  7.2 106.8 %all-gather.3.cloned.1.call-start = ((), (), s32[]{:S(2)}) async-start(), calls=%async_computation.3 | async-start | bytes 4456448 | tf_op jit(solution)/shard_map/all_gather | solution.py:31
  9.3 29.3 %all-to-all-start.1 = ((s32[2,64,2]{2,0,1:T(2,128)}), s32[2,64,2]{2,0,1:T(2,128)S(1)}, u32[]{:S(2)}, u32[]{:S(2)}) async-start(s32[2,64,2]{2,0,1:T(2,128)} %copy.192), calls=%async_computation.1 | async-start | bytes 131072 | tf_op jit(solution)/shard_map/all_to_all | solution.py:67
  39.0 74.9 %copy-start = (bf16[4,510,256]{2,0,1:T(4,128)(2,1)S(1)}, bf16[4,510,256]{2,0,1:T(4,128)(2,1)}, u32[]{:S(2)}) copy-start(bf16[4,510,256]{2,0,1:T(4,128)(2,1)} %param.8) | copy-start | bytes 3133444
  54.8 122.1 %all-to-all-start.2 = ((f32[16,2,4,2]{2,3,1,0:T(2,128)}), f32[16,2,4,2]{2,3,1,0:T(2,128)S(1)}, u32[]{:S(2)}, u32[]{:S(2)}) async-start(f32[16,2,4,2]{2,3,1,0:T(2,128)} %constant_dynamic-update-slice_fusion), calls=%async_computation.2 | async-start | bytes 65536 | tf_op jit(solution)/shard_map/all_to_all | solution.py:15
  176.9 18.8 %all-to-all-start = ((f32[16,4,4,512]{3,2,1,0:T(4,128)}), f32[16,4,4,512]{3,2,1,0:T(4,128)S(1)}, u32[]{:S(2)}, u32[]{:S(2)}) async-start(f32[16,4,4,512]{3,2,1,0:T(4,128)} %copy.184), calls=%async_computation | async-start | bytes 1048576 | tf_op jit(solution)/shard_map/all_to_all | solution.py:50
Sparse Core Ops, SparseCore 0:
  10.6 103.2 all-gather.2
